TPU v7x, 32 devices: a whole 2x2x4 slice. The times are simulated.
32 devices in a mesh: groups: 2 (over y), pool: 8 (over z, x), tp: 2 (over core).
Axes of the slice: x: 2, y: 2, z: 4, core: 2. Of those that a mesh axis runs over, the one named last changes fastest.
Arguments:
- queries: bfloat16 [4096, 8192], P(('groups', 'pool'), 'tp'), parts along dimension 0, may hold values from -10 to 10
- new_keys: bfloat16 [4096, 1024], P(('groups', 'pool'), 'tp'), parts along dimension 0, may hold values from -5 to 5
- new_values: bfloat16 [4096, 1024], P(('groups', 'pool'), 'tp'), parts along dimension 0, may hold values from -6 to 6
- key_pool: bfloat16 [2048, 16, 1024], P(('groups', 'pool'), None, 'tp'), parts along dimension 0, may hold values from -4 to 4
- value_pool: bfloat16 [2048, 16, 1024], P(('groups', 'pool'), None, 'tp'), parts along dimension 0, may hold values from -4 to 4
- page_key_scale: bfloat16 [2048, 8], P(('groups', 'pool'), 'tp'), parts along dimension 0, may hold values from 0.5 to 2
- value_scale: bfloat16 [2048, 8], P(('groups', 'pool'), 'tp'), parts along dimension 0, may hold values from 0.5 to 2
- page_owner: int32 [16, 128], P(('groups', 'pool')), parts along dimension 0, may hold values from 0 to 7, as said below
- page_slot: int32 [16, 128], P(('groups', 'pool')), parts along dimension 0, may hold values from 0 to 127, as said below
- prefix_len: int32 [16], P(('groups', 'pool')), parts along dimension 0, may hold values from 1 to 2048, 8192 in all
- dec_owner: int32 [16, 256], P(('groups', 'pool')), parts along dimension 0, may hold values from 0 to 7, as said below
- dec_slot: int32 [16, 256], P(('groups', 'pool')), parts along dimension 0, may hold values from 0 to 511, as said below
- decode_keys: bfloat16 [8192, 1024], P(('groups', 'pool'), 'tp'), parts along dimension 0, may hold values from -6 to 6
- decode_values: bfloat16 [8192, 1024], P(('groups', 'pool'), 'tp'), parts along dimension 0, may hold values from -6 to 6
Outputs:
- attended: bfloat16 [4096, 8192], P(('groups', 'pool'), 'tp'), parts along dimension 0
- decode_keys_out: bfloat16 [8192, 1024], P(('groups', 'pool'), 'tp'), parts along dimension 0
- decode_values_out: bfloat16 [8192, 1024], P(('groups', 'pool'), 'tp'), parts along dimension 0
There are 2 independent parts, one for each index of `groups`. A program takes and returns all parts, laid end to end along the dimension named above; each array names one. Nothing has to cross between parts.
Inputs may be any that keep to these rules, and one draw needn't show every extreme that they name: `page_owner`: each request has exactly 16 of its pages on every owner. `page_slot`: pages that share an owner have different slots. `dec_owner`: each request sends exactly 32 of its new rows to every decode owner. `dec_slot`: new rows that share a decode owner have different slots, and each owner's slot 511 receives a row.
All inputs are finite; a program needn't handle non-finite values. No bound on the sum of `prefix_len` on one device may be relied on, other than what follows from the above.
Results may differ from a plain program's by a relative error of at most 0.0089.
Values may be sent and summed in bfloat16 or wider, within the bound.
A program may use at most 64 MiB of HBM per device.

v0:
```python
import math

import jax
import jax.numpy as jnp
from jax import lax
from jax.sharding import PartitionSpec as P


def dequantize(codes, scales, count_of_heads):
    count, page_tok, columns = codes.shape
    spread = codes.astype(jnp.float32).reshape(
        count, page_tok, count_of_heads, columns // count_of_heads
    )
    scaled = spread * scales.astype(jnp.float32)[:, None, :, None]
    return scaled.astype(jnp.bfloat16).reshape(count * page_tok, columns)


def head_attend(query_block, pre_keys, pre_values, fresh_keys, fresh_values, length):
    factor = 1.0 / math.sqrt(query_block.shape[2])
    pre_scores = (
        jnp.einsum("tgd,kd->gtk", query_block, pre_keys, preferred_element_type=jnp.float32)
        * factor
    )
    new_scores = (
        jnp.einsum("tgd,kd->gtk", query_block, fresh_keys, preferred_element_type=jnp.float32)
        * factor
    )
    pre_seen = (jnp.arange(pre_keys.shape[0], dtype=jnp.int32) < length)[None, None, :]
    positions = jnp.arange(query_block.shape[0], dtype=jnp.int32)
    causal = (positions[:, None] >= positions[None, :])[None]
    pre_scores = jnp.where(pre_seen, pre_scores, -jnp.inf)
    new_scores = jnp.where(causal, new_scores, -jnp.inf)
    row_max = jnp.maximum(jnp.max(pre_scores, axis=2), jnp.max(new_scores, axis=2))[:, :, None]
    pre_weights = jnp.exp(pre_scores - row_max)
    new_weights = jnp.exp(new_scores - row_max)
    row_total = jnp.sum(pre_weights, axis=2) + jnp.sum(new_weights, axis=2)
    summed = jnp.einsum(
        "gtk,kd->tgd",
        pre_weights.astype(jnp.bfloat16),
        pre_values,
        preferred_element_type=jnp.float32,
    )
    summed = summed + jnp.einsum(
        "gtk,kd->tgd",
        new_weights.astype(jnp.bfloat16),
        fresh_values,
        preferred_element_type=jnp.float32,
    )
    return (summed / jnp.transpose(row_total)[:, :, None]).astype(jnp.bfloat16)


def shards(
    queries,
    new_keys,
    new_values,
    key_pool,
    value_pool,
    page_key_scale,
    value_scale,
    page_owner,
    page_slot,
    prefix_len,
    dec_owner,
    dec_slot,
    decode_keys,
    decode_values,
):
    owner_devices = lax.axis_size("pool")
    own_index = lax.axis_index("pool")
    page_count = page_owner.shape[1]
    rows_per_owner = page_count // owner_devices
    span_rows = queries.shape[0]
    rows_owner = span_rows // owner_devices
    columns = new_keys.shape[1]
    count_of_heads = page_key_scale.shape[1]
    head_dim = columns // count_of_heads
    group_size = queries.shape[1] // columns
    page_tok = key_pool.shape[1]
    all_owner, all_slot = (
        lax.all_gather(page_owner, "pool", axis=0, tiled=True),
        lax.all_gather(page_slot, "pool", axis=0, tiled=True),
    )
    matched = all_owner == own_index
    order_rank = jnp.cumsum(matched.astype(jnp.int32), axis=1) - 1
    wanted = matched[:, None, :] & (
        order_rank[:, None, :] == jnp.arange(rows_per_owner, dtype=jnp.int32)[None, :, None]
    )
    outgoing_slot = jnp.sum(jnp.where(wanted, all_slot[:, None, :], 0), axis=2).reshape(
        owner_devices * rows_per_owner
    )
    send_keys = key_pool[outgoing_slot].reshape(owner_devices, rows_per_owner, page_tok, columns)
    send_values = value_pool[outgoing_slot].reshape(
        owner_devices, rows_per_owner, page_tok, columns
    )
    outgoing_key_scale = page_key_scale[outgoing_slot].reshape(
        owner_devices, rows_per_owner, count_of_heads
    )
    send_vscale = value_scale[outgoing_slot].reshape(owner_devices, rows_per_owner, count_of_heads)
    row_owner = dec_owner[0]
    row_slot = dec_slot[0]
    positions = jnp.arange(span_rows, dtype=jnp.int32)
    same_owner = row_owner[:, None] == row_owner[None, :]
    row_rank = jnp.sum(same_owner & (positions[None, :] < positions[:, None]), axis=1)
    placed = row_owner * rows_owner + row_rank
    inverse = jnp.zeros((span_rows,), jnp.int32).at[placed].set(positions)
    push_keys = new_keys[inverse].reshape(owner_devices, rows_owner, columns)
    push_values = new_values[inverse].reshape(owner_devices, rows_owner, columns)
    push_slot = row_slot[inverse].reshape(owner_devices, rows_owner)
    received_keys, received_values, received_key_scale, received_value_scale = (
        lax.all_to_all(send_keys, "pool", split_axis=0, concat_axis=0, tiled=True),
        lax.all_to_all(send_values, "pool", split_axis=0, concat_axis=0, tiled=True),
        lax.all_to_all(outgoing_key_scale, "pool", split_axis=0, concat_axis=0, tiled=True),
        lax.all_to_all(send_vscale, "pool", split_axis=0, concat_axis=0, tiled=True),
    )
    come_keys, come_values, come_slot = (
        lax.all_to_all(push_keys, "pool", split_axis=0, concat_axis=0, tiled=True),
        lax.all_to_all(push_values, "pool", split_axis=0, concat_axis=0, tiled=True),
        lax.all_to_all(push_slot, "pool", split_axis=0, concat_axis=0, tiled=True),
    )
    my_owner = page_owner[0]
    page_pos = jnp.arange(page_count, dtype=jnp.int32)
    same_page_owner = my_owner[:, None] == my_owner[None, :]
    page_rank = jnp.sum(same_page_owner & (page_pos[None, :] < page_pos[:, None]), axis=1)
    gather_pages = my_owner * rows_per_owner + page_rank
    pre_keys = dequantize(
        received_keys.reshape(owner_devices * rows_per_owner, page_tok, columns)[gather_pages],
        received_key_scale.reshape(owner_devices * rows_per_owner, count_of_heads)[gather_pages],
        count_of_heads,
    )
    pre_values = dequantize(
        received_values.reshape(owner_devices * rows_per_owner, page_tok, columns)[gather_pages],
        received_value_scale.reshape(owner_devices * rows_per_owner, count_of_heads)[gather_pages],
        count_of_heads,
    )
    length = prefix_len[0]

    def one_head(head):
        offset = head * head_dim
        query_cols = lax.dynamic_slice_in_dim(
            queries, head * group_size * head_dim, group_size * head_dim, 1
        )
        query_block = query_cols.reshape(span_rows, group_size, head_dim)
        result = head_attend(
            query_block,
            lax.dynamic_slice_in_dim(pre_keys, offset, head_dim, 1),
            lax.dynamic_slice_in_dim(pre_values, offset, head_dim, 1),
            lax.dynamic_slice_in_dim(new_keys, offset, head_dim, 1),
            lax.dynamic_slice_in_dim(new_values, offset, head_dim, 1),
            length,
        )
        return result.reshape(span_rows, group_size * head_dim)

    per_head = lax.map(one_head, jnp.arange(count_of_heads, dtype=jnp.int32))
    attended = jnp.transpose(per_head, (1, 0, 2)).reshape(
        span_rows, count_of_heads * group_size * head_dim
    )
    flat_slot = come_slot.reshape(owner_devices * rows_owner)
    decode_keys_out = decode_keys.at[flat_slot].set(
        come_keys.reshape(owner_devices * rows_owner, columns)
    )
    decode_values_out = decode_values.at[flat_slot].set(
        come_values.reshape(owner_devices * rows_owner, columns)
    )
    return (attended, decode_keys_out, decode_values_out)


def solution(mesh):
    in_specs = (
        P(("groups", "pool"), "tp"),
        P(("groups", "pool"), "tp"),
        P(("groups", "pool"), "tp"),
        P(("groups", "pool"), None, "tp"),
        P(("groups", "pool"), None, "tp"),
        P(("groups", "pool"), "tp"),
        P(("groups", "pool"), "tp"),
        P(("groups", "pool"), None),
        P(("groups", "pool"), None),
        P(("groups", "pool")),
        P(("groups", "pool"), None),
        P(("groups", "pool"), None),
        P(("groups", "pool"), "tp"),
        P(("groups", "pool"), "tp"),
    )
    out_specs = (
        P(("groups", "pool"), "tp"),
        P(("groups", "pool"), "tp"),
        P(("groups", "pool"), "tp"),
    )
    return jax.shard_map(shards, mesh=mesh, in_specs=in_specs, out_specs=out_specs, check_vma=False)
```

profile of v0, /device:TPU:8, one launch (start us, length us, event | category | flops | bytes accessed | tf_op | source)
XLA Modules:
  0.0 276.4 jit_solution(2688377041271947166)
XLA Ops:
  2.7 17.9 %all-gather = s32[8,1,128]{2,1,0:T(1,128)S(1)} all-gather(s32[1,1,128]{2,1,0:T(1,128)S(1)} %bitcast.158), channel_id=1, replica_groups=mesh['groups'=2,'pool'=8,'tp'=2] {'pool'}, dimensions={0}, use_global_device_ids=true | all-gather | bytes 4608 | tf_op jit(solution)/shard_map/all_gather | solution.py:80
  20.9 16.1 %all-gather.1 = s32[8,1,128]{2,1,0:T(1,128)S(1)} all-gather(s32[1,1,128]{2,1,0:T(1,128)S(1)} %bitcast.157), channel_id=1, replica_groups=mesh['groups'=2,'pool'=8,'tp'=2] {'pool'}, dimensions={0}, use_global_device_ids=true | all-gather | bytes 4608 | tf_op jit(solution)/shard_map/all_gather | solution.py:81
  38.9 6.5 %all-to-all-start.1 = ((bf16[8,16,4]{1,2,0:T(4,128)(2,1)}), bf16[8,16,4]{1,2,0:T(4,128)(2,1)S(1)}, u32[]{:S(2)}, u32[]{:S(2)}) async-start(bf16[8,16,4]{1,2,0:T(4,128)(2,1)} %copy.55), calls=%async_computation.1 | async-start | bytes 16384 | tf_op jit(solution)/shard_map/all_to_all | solution.py:113
  50.5 4.7 %all-to-all-start.3 = ((bf16[8,16,4]{1,2,0:T(4,128)(2,1)}), bf16[8,16,4]{1,2,0:T(4,128)(2,1)S(1)}, u32[]{:S(2)}, u32[]{:S(2)}) async-start(bf16[8,16,4]{1,2,0:T(4,128)(2,1)} %copy.58), calls=%async_computation.3 | async-start | bytes 16384 | tf_op jit(solution)/shard_map/all_to_all | solution.py:112
  60.3 4.7 %all-to-all-start.4 = ((s32[8,1,32]{2,1,0:T(1,128)}), s32[8,1,32]{2,1,0:T(1,128)S(1)}, u32[]{:S(2)}, u32[]{:S(2)}) async-start(s32[8,1,32]{2,1,0:T(1,128)} %all_to_all.28), calls=%async_computation.4 | async-start | bytes 8192 | tf_op jit(solution)/shard_map/all_to_all | solution.py:118
  70.0 4.8 %all-to-all-start.5 = ((bf16[8,32,512]{2,1,0:T(8,128)(2,1)}), bf16[8,32,512]{2,1,0:T(8,128)(2,1)S(1)}, u32[]{:S(2)}, u32[]{:S(2)}) async-start(bf16[8,32,512]{2,1,0:T(8,128)(2,1)} %bitcast.41), calls=%async_computation.5 | async-start | bytes 524288 | tf_op jit(solution)/shard_map/all_to_all | solution.py:116
  76.7 6.1 %all-to-all-done.5 = bf16[8,32,512]{2,1,0:T(8,128)(2,1)S(1)} async-done(((bf16[8,32,512]{2,1,0:T(8,128)(2,1)}), bf16[8,32,512]{2,1,0:T(8,128)(2,1)S(1)}, u32[]{:S(2)}, u32[]{:S(2)}) %all-to-all-start.5) | async-done | bytes 262176 | tf_op jit(solution)/shard_map/all_to_all | solution.py:116
  82.8 4.5 %all-to-all-start.6 = ((bf16[8,32,512]{2,1,0:T(8,128)(2,1)}), bf16[8,32,512]{2,1,0:T(8,128)(2,1)S(1)}, u32[]{:S(2)}, u32[]{:S(2)}) async-start(bf16[8,32,512]{2,1,0:T(8,128)(2,1)} %bitcast.147), calls=%async_computation.6 | async-start | bytes 524288 | tf_op jit(solution)/shard_map/all_to_all | solution.py:117
  89.3 8.4 %all-to-all-done.6 = bf16[8,32,512]{2,1,0:T(8,128)(2,1)S(1)} async-done(((bf16[8,32,512]{2,1,0:T(8,128)(2,1)}), bf16[8,32,512]{2,1,0:T(8,128)(2,1)S(1)}, u32[]{:S(2)}, u32[]{:S(2)}) %all-to-all-start.6) | async-done | bytes 262176 | tf_op jit(solution)/shard_map/all_to_all | solution.py:117
  98.4 6.9 %all-to-all-start = ((bf16[8,16,16,512]{3,2,1,0:T(8,128)(2,1)}), bf16[8,16,16,512]{3,2,1,0:T(8,128)(2,1)}, u32[]{:S(2)}, u32[]{:S(2)}) async-start(bf16[8,16,16,512]{3,2,1,0:T(8,128)(2,1)} %bitcast.142), calls=%async_computation | async-start | bytes 4194304 | tf_op jit(solution)/shard_map/all_to_all | solution.py:111
  105.3 3.6 %gather_fusion.4 = bf16[128,16,512]{2,1,0:T(8,128)(2,1)} fusion(bf16[128,16,512]{2,1,0:T(8,128)(2,1)} %param.19, s32[1024]{0:T(1024)S(1)} %pad_clamp_fusion.2), kind=kCustom, calls=%fused_computation.4 | custom fusion | bytes 4194816 | tf_op jit(solution)/shard_map/gather | solution.py:91
  108.9 26.7 %all-to-all-done = bf16[8,16,16,512]{3,2,1,0:T(8,128)(2,1)} async-done(((bf16[8,16,16,512]{3,2,1,0:T(8,128)(2,1)}), bf16[8,16,16,512]{3,2,1,0:T(8,128)(2,1)}, u32[]{:S(2)}, u32[]{:S(2)}) %all-to-all-start) | async-done | bytes 2097184 | tf_op jit(solution)/shard_map/all_to_all | solution.py:111
  135.6 7.8 %all-to-all-start.2 = ((bf16[8,16,16,512]{3,2,1,0:T(8,128)(2,1)}), bf16[8,16,16,512]{3,2,1,0:T(8,128)(2,1)}, u32[]{:S(2)}, u32[]{:S(2)}) async-start(bf16[8,16,16,512]{3,2,1,0:T(8,128)(2,1)} %bitcast.141), calls=%async_computation.2 | async-start | bytes 4194304 | tf_op jit(solution)/shard_map/all_to_all | solution.py:110
  146.5 3.8 %scatter_fusion = bf16[512,512]{1,0:T(8,128)(2,1)} fusion(bf16[512,512]{1,0:T(8,128)(2,1)} %copy.89, s32[256]{0:T(256)S(1)} %bitcast.152, bf16[256,512]{1,0:T(8,128)(2,1)} %bitcast.145), kind=kCustom, calls=%fused_computation.12 | custom fusion | bytes 787456 | tf_op jit(solution)/shard_map/scatter | solution.py:158
  152.8 3.8 %gather_fusion.1 = bf16[128,16,512]{2,1,0:T(8,128)(2,1)} fusion(bf16[128,16,512]{2,1,0:T(8,128)(2,1)} %bitcast.19, s32[1024]{0:T(1024)S(1)} %pad_clamp_fusion.1), kind=kCustom, calls=%fused_computation.1 | custom fusion | bytes 4194816 | tf_op jit(solution)/shard_map/gather | solution.py:131
  156.6 26.9 %all-to-all-done.2 = bf16[8,16,16,512]{3,2,1,0:T(8,128)(2,1)} async-done(((bf16[8,16,16,512]{3,2,1,0:T(8,128)(2,1)}), bf16[8,16,16,512]{3,2,1,0:T(8,128)(2,1)}, u32[]{:S(2)}, u32[]{:S(2)}) %all-to-all-start.2) | async-done | bytes 2097184 | tf_op jit(solution)/shard_map/all_to_all | solution.py:110
  183.4 3.6 %gather_fusion.5 = bf16[128,16,512]{2,1,0:T(8,128)(2,1)} fusion(bf16[128,16,512]{2,1,0:T(8,128)(2,1)} %bitcast.29, s32[1024]{0:T(1024)S(1)} %pad_clamp_fusion.1), kind=kCustom, calls=%fused_computation.5 | custom fusion | bytes 4194816 | tf_op jit(solution)/shard_map/gather | solution.py:126
  189.9 4.0 %fusion.28 = (bf16[2048,512]{1,0:T(8,128)(2,1)}, bf16[2048,512]{1,0:T(8,128)(2,1)}) fusion(f32[256,8,4,128]{3,2,1,0:T(4,128)S(1)} %bitcast.139, bf16[128,16,512]{2,1,0:T(8,128)(2,1)S(1)} %copy-done.8, f32[256,8,4,128]{3,2,1,0:T(4,128)S(1)} %bitcast.138, bf16[128,16,512]{2,1,0:T(8,128)(2,1)S(1)} %copy-done.7), kind=kLoop, calls=%fused_computation.52 | loop fusion | flops 6291456 | bytes 16777216 | tf_op jit(solution)/shard_map/convert_element_type | solution.py:15
  193.9 78.5 %while.12 = (s32[]{:T(128)}, bf16[4,256,1024]{1,2,0:T(8,128)(2,1)}, s32[4]{0:T(128)S(1)}, bf16[2048,512]{1,0:T(8,128)(2,1)}, s32[]{:T(128)}, /*index=5*/bf16[204...) while((s32[]{:T(128)}, bf16[4,256,1024]{1,2,0:T(8,128)(2,1)}, ...), condition=%wide.region_8.9_spmd, body=%wide.region_3.8_spmd.sunk | while | flops 2466576384 | bytes 65930032 | solution.py:153
  197.6 4.2 %bitcast_reduce_fusion.2 = (f32[8,256]{1,0:T(8,128)S(1)}, f32[2048,256,8]{1,0,2:T(8,128)S(1)}) fusion(pred[2048]{0:T(1024)(128)(4,1)S(1)} %iota_compare_fusion.7, bf16[256,8,128]{0,2,1:T(8,128)(2,1)S(1)} %bitcast.136, bf16[2048,512]{1,0:T(8,128)(2,1)} %get-tuple-element.277, s32[]{:T(128)S(6)} %select_n.124), kind=kOutput, calls=%fused_computation.15.clone.1 | convolution fusion | flops 1086322688 | bytes 17836036 | tf_op jit(solution)/shard_map/while/body/eval_jaxpr/tgd,kd->gtk/dot_general | solution.py:21
  202.6 4.5 %fusion.60 = f32[8,256]{1,0:T(8,128)S(1)} fusion(f32[2048,256,8]{1,0,2:T(8,128)S(1)} %get-tuple-element.238, f32[8,256]{1,0:T(8,128)S(1)} %max.11, pred[2048]{0:T(1024)(128)(4,1)S(1)} %iota_compare_fusion.7), kind=kLoop, calls=%fused_computation.18.clone.1 | loop fusion | flops 16775168 | bytes 16795648 | tf_op jit(solution)/shard_map/while/body/eval_jaxpr/reduce_sum | solution.py:36
  207.0 5.1 %fusion.59 = f32[128,8,256]{2,0,1:T(8,128)S(1)} fusion(f32[2048,256,8]{1,0,2:T(8,128)S(1)} %get-tuple-element.238, f32[8,256]{1,0:T(8,128)S(1)} %max.11, pred[2048]{0:T(1024)(128)(4,1)S(1)} %iota_compare_fusion.7, bf16[2048,512]{1,0:T(8,128)(2,1)} %get-tuple-element.275, s32[]{:T(128)S(6)} %select_n.124), kind=kOutput, calls=%fused_computation.20.clone.1 | convolution fusion | flops 1090519040 | bytes 18360324 | tf_op jit(solution)/shard_map/while/body/eval_jaxpr/gtk,kd->tgd/dot_general | solution.py:37
  217.2 4.2 %bitcast_reduce_fusion.2 = (f32[8,256]{1,0:T(8,128)S(1)}, f32[2048,256,8]{1,0,2:T(8,128)S(1)}) fusion(pred[2048]{0:T(1024)(128)(4,1)S(1)} %iota_compare_fusion.7, bf16[256,8,128]{0,2,1:T(8,128)(2,1)S(1)} %bitcast.136, bf16[2048,512]{1,0:T(8,128)(2,1)} %get-tuple-element.277, s32[]{:T(128)S(6)} %select_n.124), kind=kOutput, calls=%fused_computation.15.clone.1 | convolution fusion | flops 1086322688 | bytes 17836036 | tf_op jit(solution)/shard_map/while/body/eval_jaxpr/tgd,kd->gtk/dot_general | solution.py:21
  222.2 4.5 %fusion.60 = f32[8,256]{1,0:T(8,128)S(1)} fusion(f32[2048,256,8]{1,0,2:T(8,128)S(1)} %get-tuple-element.238, f32[8,256]{1,0:T(8,128)S(1)} %max.11, pred[2048]{0:T(1024)(128)(4,1)S(1)} %iota_compare_fusion.7), kind=kLoop, calls=%fused_computation.18.clone.1 | loop fusion | flops 16775168 | bytes 16795648 | tf_op jit(solution)/shard_map/while/body/eval_jaxpr/reduce_sum | solution.py:36
  226.7 5.1 %fusion.59 = f32[128,8,256]{2,0,1:T(8,128)S(1)} fusion(f32[2048,256,8]{1,0,2:T(8,128)S(1)} %get-tuple-element.238, f32[8,256]{1,0:T(8,128)S(1)} %max.11, pred[2048]{0:T(1024)(128)(4,1)S(1)} %iota_compare_fusion.7, bf16[2048,512]{1,0:T(8,128)(2,1)} %get-tuple-element.275, s32[]{:T(128)S(6)} %select_n.124), kind=kOutput, calls=%fused_computation.20.clone.1 | convolution fusion | flops 1090519040 | bytes 18360324 | tf_op jit(solution)/shard_map/while/body/eval_jaxpr/gtk,kd->tgd/dot_general | solution.py:37
  236.8 4.2 %bitcast_reduce_fusion.2 = (f32[8,256]{1,0:T(8,128)S(1)}, f32[2048,256,8]{1,0,2:T(8,128)S(1)}) fusion(pred[2048]{0:T(1024)(128)(4,1)S(1)} %iota_compare_fusion.7, bf16[256,8,128]{0,2,1:T(8,128)(2,1)S(1)} %bitcast.136, bf16[2048,512]{1,0:T(8,128)(2,1)} %get-tuple-element.277, s32[]{:T(128)S(6)} %select_n.124), kind=kOutput, calls=%fused_computation.15.clone.1 | convolution fusion | flops 1086322688 | bytes 17836036 | tf_op jit(solution)/shard_map/while/body/eval_jaxpr/tgd,kd->gtk/dot_general | solution.py:21
  241.8 4.5 %fusion.60 = f32[8,256]{1,0:T(8,128)S(1)} fusion(f32[2048,256,8]{1,0,2:T(8,128)S(1)} %get-tuple-element.238, f32[8,256]{1,0:T(8,128)S(1)} %max.11, pred[2048]{0:T(1024)(128)(4,1)S(1)} %iota_compare_fusion.7), kind=kLoop, calls=%fused_computation.18.clone.1 | loop fusion | flops 16775168 | bytes 16795648 | tf_op jit(solution)/shard_map/while/body/eval_jaxpr/reduce_sum | solution.py:36
  246.3 5.1 %fusion.59 = f32[128,8,256]{2,0,1:T(8,128)S(1)} fusion(f32[2048,256,8]{1,0,2:T(8,128)S(1)} %get-tuple-element.238, f32[8,256]{1,0:T(8,128)S(1)} %max.11, pred[2048]{0:T(1024)(128)(4,1)S(1)} %iota_compare_fusion.7, bf16[2048,512]{1,0:T(8,128)(2,1)} %get-tuple-element.275, s32[]{:T(128)S(6)} %select_n.124), kind=kOutput, calls=%fused_computation.20.clone.1 | convolution fusion | flops 1090519040 | bytes 18360324 | tf_op jit(solution)/shard_map/while/body/eval_jaxpr/gtk,kd->tgd/dot_general | solution.py:37
  256.4 4.2 %bitcast_reduce_fusion.2 = (f32[8,256]{1,0:T(8,128)S(1)}, f32[2048,256,8]{1,0,2:T(8,128)S(1)}) fusion(pred[2048]{0:T(1024)(128)(4,1)S(1)} %iota_compare_fusion.7, bf16[256,8,128]{0,2,1:T(8,128)(2,1)S(1)} %bitcast.136, bf16[2048,512]{1,0:T(8,128)(2,1)} %get-tuple-element.277, s32[]{:T(128)S(6)} %select_n.124), kind=kOutput, calls=%fused_computation.15.clone.1 | convolution fusion | flops 1086322688 | bytes 17836036 | tf_op jit(solution)/shard_map/while/body/eval_jaxpr/tgd,kd->gtk/dot_general | solution.py:21
  261.4 4.5 %fusion.60 = f32[8,256]{1,0:T(8,128)S(1)} fusion(f32[2048,256,8]{1,0,2:T(8,128)S(1)} %get-tuple-element.238, f32[8,256]{1,0:T(8,128)S(1)} %max.11, pred[2048]{0:T(1024)(128)(4,1)S(1)} %iota_compare_fusion.7), kind=kLoop, calls=%fused_computation.18.clone.1 | loop fusion | flops 16775168 | bytes 16795648 | tf_op jit(solution)/shard_map/while/body/eval_jaxpr/reduce_sum | solution.py:36
  265.9 5.1 %fusion.59 = f32[128,8,256]{2,0,1:T(8,128)S(1)} fusion(f32[2048,256,8]{1,0,2:T(8,128)S(1)} %get-tuple-element.238, f32[8,256]{1,0:T(8,128)S(1)} %max.11, pred[2048]{0:T(1024)(128)(4,1)S(1)} %iota_compare_fusion.7, bf16[2048,512]{1,0:T(8,128)(2,1)} %get-tuple-element.275, s32[]{:T(128)S(6)} %select_n.124), kind=kOutput, calls=%fused_computation.20.clone.1 | convolution fusion | flops 1090519040 | bytes 18360324 | tf_op jit(solution)/shard_map/while/body/eval_jaxpr/gtk,kd->tgd/dot_general | solution.py:37
  272.4 4.1 %copy.68 = bf16[256,4096]{1,0:T(8,128)(2,1)} copy(bf16[256,4096]{0,1:T(8,128)(2,1)} %bitcast.34) | data formatting | bytes 4194304 | tf_op jit(solution)/shard_map/reshape | solution.py:154
  (126 shorter events, 50.8 us)
Async XLA Ops:
  0.6 86.7 %copy-start = (bf16[128,16,512]{2,1,0:T(8,128)(2,1)S(1)}, bf16[128,16,512]{2,1,0:T(8,128)(2,1)}, u32[]{:S(2)}) copy-start(bf16[128,16,512]{2,1,0:T(8,128)(2,1)} %param.20) | copy-start | bytes 6291460
  0.6 64.4 %copy-start.2 = (bf16[256,512]{1,0:T(8,128)(2,1)S(1)}, bf16[256,512]{1,0:T(8,128)(2,1)}, u32[]{:S(2)}) copy-start(bf16[256,512]{1,0:T(8,128)(2,1)} %param.17) | copy-start | bytes 786436
  0.7 46.5 %copy-start.13 = (bf16[128,4]{0,1:T(4,128)(2,1)S(1)}, bf16[128,4]{0,1:T(4,128)(2,1)}, u32[]{:S(2)}) copy-start(bf16[128,4]{0,1:T(4,128)(2,1)} %param.21) | copy-start | bytes 3076
  0.7 36.7 %copy-start.12 = (bf16[128,4]{0,1:T(4,128)(2,1)S(1)}, bf16[128,4]{0,1:T(4,128)(2,1)}, u32[]{:S(2)}) copy-start(bf16[128,4]{0,1:T(4,128)(2,1)} %param.22) | copy-start | bytes 3076
  0.7 2.1 copy-start.15
  0.7 20.2 %copy-start.14 = (s32[1,128]{1,0:T(1,128)S(1)}, s32[1,128]{1,0:T(1,128)}, u32[]{:S(2)}) copy-start(s32[1,128]{1,0:T(1,128)} %param.24) | copy-start | bytes 1540
  0.7 44.8 %copy-start.11 = (s32[1,256]{1,0:T(1,128)S(1)}, s32[1,256]{1,0:T(1,128)}, u32[]{:S(2)}) copy-start(s32[1,256]{1,0:T(1,128)} %param.26) | copy-start | bytes 3076
  0.7 54.6 %copy-start.1 = (s32[1,256]{1,0:T(1,128)S(1)}, s32[1,256]{1,0:T(1,128)}, u32[]{:S(2)}) copy-start(s32[1,256]{1,0:T(1,128)} %param.27) | copy-start | bytes 3076
  38.9 11.6 %all-to-all-start.1 = ((bf16[8,16,4]{1,2,0:T(4,128)(2,1)}), bf16[8,16,4]{1,2,0:T(4,128)(2,1)S(1)}, u32[]{:S(2)}, u32[]{:S(2)}) async-start(bf16[8,16,4]{1,2,0:T(4,128)(2,1)} %copy.55), calls=%async_computation.1 | async-start | bytes 16384 | tf_op jit(solution)/shard_map/all_to_all | solution.py:113
  47.3 27.6 %copy-start.3 = (bf16[256,512]{1,0:T(8,128)(2,1)S(1)}, bf16[256,512]{1,0:T(8,128)(2,1)}, u32[]{:S(2)}) copy-start(bf16[256,512]{1,0:T(8,128)(2,1)} %param.18) | copy-start | bytes 786436
  50.5 9.8 %all-to-all-start.3 = ((bf16[8,16,4]{1,2,0:T(4,128)(2,1)}), bf16[8,16,4]{1,2,0:T(4,128)(2,1)S(1)}, u32[]{:S(2)}, u32[]{:S(2)}) async-start(bf16[8,16,4]{1,2,0:T(4,128)(2,1)} %copy.58), calls=%async_computation.3 | async-start | bytes 16384 | tf_op jit(solution)/shard_map/all_to_all | solution.py:112
  60.3 9.7 %all-to-all-start.4 = ((s32[8,1,32]{2,1,0:T(1,128)}), s32[8,1,32]{2,1,0:T(1,128)S(1)}, u32[]{:S(2)}, u32[]{:S(2)}) async-start(s32[8,1,32]{2,1,0:T(1,128)} %all_to_all.28), calls=%async_computation.4 | async-start | bytes 8192 | tf_op jit(solution)/shard_map/all_to_all | solution.py:118
  70.0 12.8 %all-to-all-start.5 = ((bf16[8,32,512]{2,1,0:T(8,128)(2,1)}), bf16[8,32,512]{2,1,0:T(8,128)(2,1)S(1)}, u32[]{:S(2)}, u32[]{:S(2)}) async-start(bf16[8,32,512]{2,1,0:T(8,128)(2,1)} %bitcast.41), calls=%async_computation.5 | async-start | bytes 524288 | tf_op jit(solution)/shard_map/all_to_all | solution.py:116
  82.8 6.5 %copy-start.9 = (bf16[8,32,512]{2,1,0:T(8,128)(2,1)}, bf16[8,32,512]{2,1,0:T(8,128)(2,1)S(1)}, u32[]{:S(2)}) copy-start(bf16[8,32,512]{2,1,0:T(8,128)(2,1)S(1)} %all-to-all-done.5) | copy-start | bytes 786436
  82.8 14.9 %all-to-all-start.6 = ((bf16[8,32,512]{2,1,0:T(8,128)(2,1)}), bf16[8,32,512]{2,1,0:T(8,128)(2,1)S(1)}, u32[]{:S(2)}, u32[]{:S(2)}) async-start(bf16[8,32,512]{2,1,0:T(8,128)(2,1)} %bitcast.147), calls=%async_computation.6 | async-start | bytes 524288 | tf_op jit(solution)/shard_map/all_to_all | solution.py:117
  97.7 0.7 copy-start.10
  98.4 37.1 %all-to-all-start = ((bf16[8,16,16,512]{3,2,1,0:T(8,128)(2,1)}), bf16[8,16,16,512]{3,2,1,0:T(8,128)(2,1)}, u32[]{:S(2)}, u32[]{:S(2)}) async-start(bf16[8,16,16,512]{3,2,1,0:T(8,128)(2,1)} %bitcast.142), calls=%async_computation | async-start | bytes 4194304 | tf_op jit(solution)/shard_map/all_to_all | solution.py:111
  135.6 47.9 %all-to-all-start.2 = ((bf16[8,16,16,512]{3,2,1,0:T(8,128)(2,1)}), bf16[8,16,16,512]{3,2,1,0:T(8,128)(2,1)}, u32[]{:S(2)}, u32[]{:S(2)}) async-start(bf16[8,16,16,512]{3,2,1,0:T(8,128)(2,1)} %bitcast.141), calls=%async_computation.2 | async-start | bytes 4194304 | tf_op jit(solution)/shard_map/all_to_all | solution.py:110
  146.5 3.8 %copy-start.6 = (bf16[512,512]{1,0:T(8,128)(2,1)S(1)}, bf16[512,512]{1,0:T(8,128)(2,1)}, u32[]{:S(2)}) copy-start(bf16[512,512]{1,0:T(8,128)(2,1)} %param.29) | copy-start | bytes 1572868
  152.8 3.8 %copy-start.5 = (bf16[512,512]{1,0:T(8,128)(2,1)}, bf16[512,512]{1,0:T(8,128)(2,1)S(1)}, u32[]{:S(2)}) copy-start(bf16[512,512]{1,0:T(8,128)(2,1)S(1)} %scatter_fusion.1) | copy-start | bytes 1572868
  187.6 1.6 copy-start.7
  187.6 2.2 copy-start.8
  207.0 5.1 %copy-start.4 = (bf16[256,512]{1,0:T(8,128)(2,1)S(1)}, bf16[256,512]{1,0:T(8,128)(2,1)}, u32[]{:S(2)}) copy-start(bf16[256,512]{1,0:T(8,128)(2,1)} %get-tuple-element.302) | copy-start | bytes 786436 | tf_op jit(solution)/shard_map/while
  226.6 5.1 %copy-start.4 = (bf16[256,512]{1,0:T(8,128)(2,1)S(1)}, bf16[256,512]{1,0:T(8,128)(2,1)}, u32[]{:S(2)}) copy-start(bf16[256,512]{1,0:T(8,128)(2,1)} %get-tuple-element.302) | copy-start | bytes 786436 | tf_op jit(solution)/shard_map/while
  246.3 5.1 %copy-start.4 = (bf16[256,512]{1,0:T(8,128)(2,1)S(1)}, bf16[256,512]{1,0:T(8,128)(2,1)}, u32[]{:S(2)}) copy-start(bf16[256,512]{1,0:T(8,128)(2,1)} %get-tuple-element.302) | copy-start | bytes 786436 | tf_op jit(solution)/shard_map/while
  265.9 5.1 %copy-start.4 = (bf16[256,512]{1,0:T(8,128)(2,1)S(1)}, bf16[256,512]{1,0:T(8,128)(2,1)}, u32[]{:S(2)}) copy-start(bf16[256,512]{1,0:T(8,128)(2,1)} %get-tuple-element.302) | copy-start | bytes 786436 | tf_op jit(solution)/shard_map/while
where the time goes:
time: 282 us; the launch traced here: 276 us
  waiting for transfers between devices  75.4 us (27%)
  local copies, waits for them, and re-layouts  52.9 us (19%)
  matrix products  40.9 us (15%)
  starting transfers between devices  40 us (14%)
  blocking collectives  34 us (12%)
  other arithmetic  27.3 us (10%)
  loops' own time  4.96 us (2%)
    all_to_all x1, waiting for transfers between devices, shards(): lax.all_to_all(send_keys, 'pool', split_axis=0, concat_axis=0, tiled=True)  26.9 us
    all_to_all x1, waiting for transfers between devices, shards(): lax.all_to_all(send_values, 'pool', split_axis=0, concat_axis=0, tiled=True)  26.7 us
    dot_general x4, matrix products, head_attend(): jnp.einsum('gtk,kd->tgd', pre_weights.astype(jnp.bfloat16), pre_values, p...  20.2 us
    reduce_sum x8, other arithmetic, head_attend(): row_total = jnp.sum(pre_weights, axis=2) + jnp.sum(new_weights, axis=2)  19 us
    all_gather x1, blocking collectives, shards(): lax.all_gather(page_owner, 'pool', axis=0, tiled=True)  17.9 us
    dot_general x4, matrix products, head_attend(): jnp.einsum('tgd,kd->gtk', query_block, pre_keys, preferred_element_type=j...  16.8 us
    all_gather x1, blocking collectives, shards(): lax.all_gather(page_slot, 'pool', axis=0, tiled=True)  16.1 us
    all_to_all x1, waiting for transfers between devices, shards(): lax.all_to_all(push_values, 'pool', split_axis=0, concat_axis=0, tiled=True)  8.39 us
  transfers between devices with their start and end apart: 7, of which 7 were waited for; matrix products, arithmetic and copies ran while one was open for 10% of the time, Pallas kernels for 0%

commit v1 on v0

v1 whole, which is shorter than its diff:
```python
import functools
import math

import jax
import jax.numpy as jnp
from jax import lax
from jax.experimental import pallas as pl
from jax.experimental.pallas import tpu as pltpu
from jax.sharding import PartitionSpec as P

MESH = pl.DeviceIdType.MESH
LOW = -1e30
TABLE_ROWS_AT = 64
UNROLL = 4


def flipped(me, d):
    out = me
    bit = 1
    while bit <= d:
        if d & bit:
            out = out + bit - 2 * bit * lax.rem(lax.div(me, bit), 2)
        bit *= 2
    return out


def send_order(n):
    top = n // 2
    order = []
    while top >= 1:
        order += list(range(top, 2 * top))
        top //= 2
    return order


def kernel(
    n,
    rows,
    page_tok,
    dec_rows,
    dec_pad,
    kv_heads,
    group,
    tab_ref,
    placed_ref,
    q_ref,
    nk_ref,
    nv_ref,
    kp_ref,
    vp_ref,
    ks_ref,
    vs_ref,
    bias_ref,
    out_ref,
    come_ref,
    tabin_ref,
    tab_smem,
    stage,
    recv,
    push,
    acc,
    m_ref,
    l_ref,
    tsend,
    trecv,
    psend,
    precv,
    dsend,
    drecv,
    lsem,
):
    me = lax.axis_index("pool")
    keys = rows * page_tok
    span = q_ref.shape[0]
    heads = kv_heads * group
    hd = q_ref.shape[1] // heads
    order = send_order(n)

    barrier = pltpu.get_barrier_semaphore()
    for d in range(1, n):
        pl.semaphore_signal(barrier, inc=1, device_id={"pool": flipped(me, d)}, device_id_type=MESH)
    pl.semaphore_wait(barrier, n - 1)

    def table_copy(d):
        p = flipped(me, d)
        return pltpu.make_async_remote_copy(
            src_ref=tab_ref.at[p],
            dst_ref=tabin_ref.at[me],
            send_sem=tsend.at[d],
            recv_sem=trecv.at[d],
            device_id={"pool": p},
            device_id_type=MESH,
        )

    def page_copy(d):
        return pltpu.make_async_remote_copy(
            src_ref=stage.at[d],
            dst_ref=recv.at[:, pl.ds(pl.multiple_of(me * keys, keys), keys)],
            send_sem=psend.at[d],
            recv_sem=precv.at[d],
            device_id={"pool": flipped(me, d)},
            device_id_type=MESH,
        )

    def row_copy(d):
        p = flipped(me, d)
        return pltpu.make_async_remote_copy(
            src_ref=push.at[p],
            dst_ref=come_ref.at[me],
            send_sem=dsend.at[d],
            recv_sem=drecv.at[d],
            device_id={"pool": p},
            device_id_type=MESH,
        )

    for d in order:
        table_copy(d).start()
    tabin_ref[me] = tab_ref[me]
    for d in order:
        table_copy(d).wait_recv()
    to_smem = pltpu.make_async_copy(tabin_ref, tab_smem, lsem)
    to_smem.start()
    to_smem.wait()

    def gather(p, write):
        def one(k, carry):
            slot = tab_smem[p, 0, k]
            at = pl.multiple_of(k * page_tok, page_tok)
            key_page = kp_ref[slot].astype(jnp.float32) * ks_ref[slot]
            value_page = vp_ref[slot].astype(jnp.float32) * vs_ref[slot]
            write(at, key_page.astype(jnp.bfloat16), value_page.astype(jnp.bfloat16))
            return carry

        lax.fori_loop(0, rows, one, 0, unroll=True)

    for d in order:

        def to_stage(at, key_page, value_page):
            stage[d, 0, pl.ds(at, page_tok)] = key_page
            stage[d, 1, pl.ds(at, page_tok)] = value_page

        gather(flipped(me, d), to_stage)
        page_copy(d).start()

    def to_own(at, key_page, value_page):
        base = pl.multiple_of(me * keys, keys)
        recv[0, pl.ds(base + at, page_tok)] = key_page
        recv[1, pl.ds(base + at, page_tok)] = value_page

    gather(me, to_own)

    for o in range(n):
        spot = lax.broadcasted_iota(jnp.int32, (dec_pad, span), 0) + o * dec_pad
        placed = placed_ref[...]
        pick_k = jnp.where(spot == placed, 1.0, 0.0).astype(jnp.bfloat16)
        pick_v = jnp.where(spot == placed + dec_rows, 1.0, 0.0).astype(jnp.bfloat16)
        push[o] = (
            jnp.dot(pick_k, nk_ref[...], preferred_element_type=jnp.float32)
            + jnp.dot(pick_v, nv_ref[...], preferred_element_type=jnp.float32)
        ).astype(jnp.bfloat16)
    come_ref[me] = push[me]
    for d in order:
        row_copy(d).start()

    scale = math.log2(math.e) / math.sqrt(hd)

    def attend(load_k, load_v, load_bias, first):
        def some_heads(i, carry):
            for u in range(UNROLL):
                c = i * UNROLL + u
                h = lax.div(i * UNROLL, group)
                col = pl.multiple_of(h * hd, hd)
                q = q_ref[:, pl.ds(pl.multiple_of(c * hd, hd), hd)]
                s = lax.dot_general(
                    load_k(col), q, (((1,), (1,)), ((), ())), preferred_element_type=jnp.float32
                )
                s = s + load_bias()
                top = jnp.max(s, axis=0, keepdims=True)
                if not first:
                    old = m_ref[c]
                    top = jnp.maximum(old, top)
                w = jnp.exp2((s - top) * scale)
                part = jnp.sum(w.reshape(w.shape[0] // 8, 8, span), axis=0)
                summed = lax.dot_general(
                    load_v(col),
                    w.astype(jnp.bfloat16),
                    (((0,), (0,)), ((), ())),
                    preferred_element_type=jnp.float32,
                )
                if first:
                    l_ref[c] = part
                    acc[c] = summed
                else:
                    fade = jnp.exp2((old - top) * scale)
                    l_ref[c] = l_ref[c] * fade + part
                    acc[c] = acc[c] * fade + summed
                m_ref[c] = top
            return carry

        lax.fori_loop(0, heads // UNROLL, some_heads, 0)

    def causal():
        s_at = lax.broadcasted_iota(jnp.int32, (span, span), 0)
        t_at = lax.broadcasted_iota(jnp.int32, (span, span), 1)
        return jnp.where(s_at <= t_at, 0.0, LOW)

    attend(lambda col: nk_ref[:, pl.ds(col, hd)], lambda col: nv_ref[:, pl.ds(col, hd)], causal, True)

    per_block = max(1, 256 // keys)
    block = per_block * keys
    own_block = lax.div(me, per_block)
    done = {0}
    for i in [0] + send_order(n // per_block):
        for d in range(i * per_block, (i + 1) * per_block):
            if d:
                page_copy(d).wait_recv()
        base = pl.multiple_of(flipped(own_block, i) * block, block)

        def bias_block():
            b = bias_ref[pl.ds(base, block), :]
            return jnp.concatenate([b] * (span // b.shape[1]), axis=1)

        attend(
            lambda col: recv[0, pl.ds(base, block), pl.ds(col, hd)],
            lambda col: recv[1, pl.ds(base, block), pl.ds(col, hd)],
            bias_block,
            False,
        )

    def finish(c, carry):
        total = jnp.sum(l_ref[c], axis=0, keepdims=True)
        value = acc[c] / total
        out_ref[:, pl.ds(pl.multiple_of(c * hd, hd), hd)] = value.T.astype(jnp.bfloat16)
        return carry

    lax.fori_loop(0, heads, finish, 0)

    for d in order:
        table_copy(d).wait_send()
        page_copy(d).wait_send()
        row_copy(d).wait()


def ranks(owner):
    at = jnp.arange(owner.shape[0], dtype=jnp.int32)
    same = owner[:, None] == owner[None, :]
    return jnp.sum(same & (at[None, :] < at[:, None]), axis=1, dtype=jnp.int32)


def shards(
    queries,
    new_keys,
    new_values,
    key_pool,
    value_pool,
    page_key_scale,
    value_scale,
    page_owner,
    page_slot,
    prefix_len,
    dec_owner,
    dec_slot,
    decode_keys,
    decode_values,
):
    n = lax.axis_size("pool")
    page_count = page_owner.shape[1]
    rows = page_count // n
    span = queries.shape[0]
    dec_rows = span // n
    dec_pad = -(-2 * dec_rows // 16) * 16
    columns = new_keys.shape[1]
    kv_heads = page_key_scale.shape[1]
    hd = columns // kv_heads
    group = queries.shape[1] // columns
    pool_pages, page_tok, _ = key_pool.shape
    keys = rows * page_tok

    owner, slot = page_owner[0], page_slot[0]
    place = owner * rows + ranks(owner)
    hit = place[None, :] == jnp.arange(page_count, dtype=jnp.int32)[:, None]
    slots = jnp.sum(jnp.where(hit, slot[None, :], 0), axis=1).reshape(n, rows)
    pages = jnp.sum(
        jnp.where(hit, jnp.arange(page_count, dtype=jnp.int32)[None, :], 0), axis=1
    )
    position = pages[:, None] * page_tok + jnp.arange(page_tok, dtype=jnp.int32)[None, :]
    bias = jnp.where(position.reshape(page_count * page_tok) < prefix_len[0], 0.0, LOW)
    bias = jnp.broadcast_to(bias.astype(jnp.float32)[:, None], (page_count * page_tok, 128))

    d_owner, d_slot = dec_owner[0], dec_slot[0]
    d_rank = ranks(d_owner)
    d_hit = (d_owner * dec_rows + d_rank)[None, :] == jnp.arange(span, dtype=jnp.int32)[:, None]
    d_slots = jnp.sum(jnp.where(d_hit, d_slot[None, :], 0), axis=1).reshape(n, dec_rows)
    placed = (d_owner * dec_pad + d_rank)[None, :]

    table = jnp.concatenate(
        [
            slots,
            jnp.zeros((n, TABLE_ROWS_AT - rows), jnp.int32),
            d_slots,
            jnp.zeros((n, 128 - TABLE_ROWS_AT - dec_rows), jnp.int32),
        ],
        axis=1,
    ).reshape(n, 1, 128)
    key_scale = jnp.repeat(page_key_scale.astype(jnp.float32), hd, axis=1)[:, None, :]
    val_scale = jnp.repeat(value_scale.astype(jnp.float32), hd, axis=1)[:, None, :]

    heads = kv_heads * group
    vmem = pl.BlockSpec(memory_space=pltpu.VMEM)
    attended, come, table_in = pl.pallas_call(
        functools.partial(
            kernel, n, rows, page_tok, dec_rows, dec_pad, kv_heads, group
        ),
        out_shape=(
            jax.ShapeDtypeStruct(queries.shape, jnp.bfloat16),
            jax.ShapeDtypeStruct((n, dec_pad, columns), jnp.bfloat16),
            jax.ShapeDtypeStruct((n, 1, 128), jnp.int32),
        ),
        in_specs=[vmem] * 10,
        out_specs=(vmem, vmem, vmem),
        scratch_shapes=[
            pltpu.SMEM((n, 1, 128), jnp.int32),
            pltpu.VMEM((n, 2, keys, columns), jnp.bfloat16),
            pltpu.VMEM((2, n * keys, columns), jnp.bfloat16),
            pltpu.VMEM((n, dec_pad, columns), jnp.bfloat16),
            pltpu.VMEM((heads, hd, span), jnp.float32),
            pltpu.VMEM((heads, 1, span), jnp.float32),
            pltpu.VMEM((heads, 8, span), jnp.float32),
            pltpu.SemaphoreType.DMA((n,)),
            pltpu.SemaphoreType.DMA((n,)),
            pltpu.SemaphoreType.DMA((n,)),
            pltpu.SemaphoreType.DMA((n,)),
            pltpu.SemaphoreType.DMA((n,)),
            pltpu.SemaphoreType.DMA((n,)),
            pltpu.SemaphoreType.DMA,
        ],
        compiler_params=pltpu.CompilerParams(
            collective_id=0, has_side_effects=True, vmem_limit_bytes=52 * 1024 * 1024
        ),
        cost_estimate=pl.CostEstimate(
            flops=4 * span * heads * hd * (n * keys + span),
            bytes_accessed=16 * 1024 * 1024,
            transcendentals=span * heads * (n * keys + span),
        ),
    )(
        table,
        placed,
        queries,
        new_keys,
        new_values,
        key_pool,
        value_pool,
        key_scale,
        val_scale,
        bias,
    )

    come_slot = table_in[:, 0, TABLE_ROWS_AT : TABLE_ROWS_AT + dec_rows].reshape(span)
    put = jnp.arange(decode_keys.shape[0], dtype=jnp.int32)[:, None] == come_slot[None, :]
    touched = jnp.any(put, axis=1)[:, None]
    put = put.astype(jnp.bfloat16)
    come_keys = come[:, :dec_rows].reshape(span, columns)
    come_values = come[:, dec_rows : 2 * dec_rows].reshape(span, columns)
    keys_out = jnp.where(
        touched,
        jnp.dot(put, come_keys, preferred_element_type=jnp.float32).astype(jnp.bfloat16),
        decode_keys,
    )
    values_out = jnp.where(
        touched,
        jnp.dot(put, come_values, preferred_element_type=jnp.float32).astype(jnp.bfloat16),
        decode_values,
    )
    return attended, keys_out, values_out


def solution(mesh):
    two = P(("groups", "pool"), "tp")
    three = P(("groups", "pool"), None, "tp")
    table = P(("groups", "pool"), None)
    in_specs = (two, two, two, three, three, two, two, table, table)
    in_specs += (P(("groups", "pool")), table, table, two, two)
    return jax.shard_map(
        shards, mesh=mesh, in_specs=in_specs, out_specs=(two, two, two), check_vma=False
    )
```

time: 282 us -> 172 us (0.61); the launches traced: 276 us -> 172 us
  Pallas kernels: 0 us -> 155 us
  waiting for transfers between devices: 75.4 us -> 0 us
  local copies, waits for them, and re-layouts: 52.9 us -> 7.12 us
  starting transfers between devices: 40 us -> 0 us
  matrix products: 40.9 us -> 3.26 us
  blocking collectives: 34 us -> 0 us
  other arithmetic: 27.3 us -> 5.07 us
  loops' own time: 4.96 us -> 0 us
    pallas_call x0 -> x1, Pallas kernels: none -> 155 us  [shards(): pl.pallas_call(functools.partial(kernel, n, rows, page_tok, dec_rows, dec...]
    all_to_all x7 -> x0, waiting for transfers between devices: 75.4 us -> none  [the longest x1 26.9 us: shards(): lax.all_to_all(send_keys, 'pool', split_axis=0, concat_axis=0, tiled=True)]
    all_to_all x7 -> x0, starting transfers between devices: 40 us -> none  [the longest x1 7.79 us: shards(): lax.all_to_all(send_keys, 'pool', split_axis=0, concat_axis=0, tiled=True)]
    dot_general x16 -> x2, matrix products: 40.9 us -> 3.26 us  [the longest x1 2.15 us: shards(): jnp.dot(put, come_values, preferred_element_type=jnp.float32)]
    all_gather x2 -> x0, blocking collectives: 34 us -> none  [the longest x1 17.9 us: shards(): lax.all_gather(page_owner, 'pool', axis=0, tiled=True)]
    gather x11 -> x0, local copies, waits for them, and re-layouts: 21.5 us -> none  [the longest x1 3.81 us: shards(): received_values.reshape(owner_devices * rows_per_owner, page_tok, columns)]
    reduce_sum x11 -> x4, other arithmetic: 19.6 us -> 3.38 us  [the longest x2 1.83 us: ranks(): return jnp.sum(same & (at[None, :] < at[:, None]), axis=1, dtype=jnp.int32)]
    scatter x3 -> x0, local copies, waits for them, and re-layouts: 7.59 us -> none  [the longest x1 3.82 us: shards(): decode_keys.at[flat_slot]]
  transfers between devices with their start and end apart: 7 -> 0, of which waited for: 7 -> 0; matrix products, arithmetic and copies ran while one was open for 10% -> 0% of each run, Pallas kernels for 0% -> 0%
where the time goes in v1:
time: 172 us
  Pallas kernels  155 us (90%)
  local copies, waits for them, and re-layouts  7.12 us (4%)
  other arithmetic  5.07 us (3%)
  matrix products  3.26 us (2%)
    pallas_call x1, Pallas kernels, shards(): pl.pallas_call(functools.partial(kernel, n, rows, page_tok, dec_rows, dec...  155 us

profile of v1, /device:TPU:8, one launch (start us, length us, event | category | flops | bytes accessed | tf_op | source)
XLA Modules:
  0.0 171.9 jit_solution(18083399875718092423)
XLA Ops:
  1.3 0.9 convert_reduce_fusion.1
  2.2 0.7 fusion.8
  2.9 0.1 pad.1.clone
  2.9 0.1 pad.3.clone
  3.0 0.8 select_reduce_fusion.1
  3.8 0.9 convert_reduce_fusion
  4.7 0.7 multiply_add_fusion
  5.4 0.8 select_reduce_fusion
  6.2 0.1 reshape.53
  6.3 0.1 reshape.52
  6.4 0.1 add_add_fusion
  6.4 0.1 fusion.7
  6.5 0.1 select_n.33
  6.6 0.8 copy.21
  7.4 0.8 copy.22
  8.2 0.2 broadcast_in_dim.92
  8.4 0.2 broadcast_in_dim.91
  8.6 1.3 broadcast_in_dim.95.bias_ref
  9.9 0.0 copy-start
  9.9 0.9 copy-done
  10.9 0.0 copy-start.1
  10.9 0.9 copy-done.1
  11.8 155.1 %shard_map.157 = (bf16[256,4096]{1,0:T(8,128)(2,1)}, bf16[8,64,512]{2,1,0:T(8,128)(2,1)S(1)}, s32[8,1,128]{2,1,0:T(1,128)S(1)}) custom-call(s32[8,1,128]{2,1,0:T(1,128)S(1)} %bitcast.23, s32[1,256]{1,0:T(1,128)S(1)} %get-tuple-element.13.placed_ref, bf16[256,4096]{1,0:T(8,128)(2,1)} %q_ref.1, bf16[256,512]{1,0:T(8,128)(2,1)S(1)} %copy-done, ...), custom_call_target="tpu_custom_call" | custom-call | flops 9663676416 | bytes 16777216 | tf_op jit(solution)/shard_map/pallas_call | solution.py:310
  166.9 0.0 copy-start.2
  166.9 0.1 slice_reduce_fusion
  167.0 0.1 eq.86
  167.1 0.2 fusion.2
  167.3 0.0 copy-done.3
  167.3 1.1 fusion
  168.4 2.2 %fusion.1 = bf16[512,512]{1,0:T(8,128)(2,1)} fusion(bf16[512,512]{1,0:T(8,128)(2,1)} %param.27, bf16[256,512]{1,0:T(8,128)(2,1)S(1)} %bitcast.24, pred[512]{0:T(512)(128)(4,1)S(1)} %fusion.2, s32[256]{0:T(256)S(1)} %eq.86), kind=kOutput, calls=%fused_computation.3 | convolution fusion | flops 134873088 | bytes 1312256 | tf_op jit(solution)/shard_map/dot_general | solution.py:371
  170.6 0.0 copy-done.2
  170.6 1.3 copy.25
  (5 shorter events, 0.1 us)
Async XLA Ops:
  9.9 0.9 copy-start
  10.9 0.9 copy-start.1
  11.8 155.5 %copy-start.3 = (bf16[512,512]{1,0:T(8,128)(2,1)S(1)}, bf16[512,512]{1,0:T(8,128)(2,1)}, u32[]{:S(2)}) copy-start(bf16[512,512]{1,0:T(8,128)(2,1)} %param.26) | copy-start | bytes 1572868
  166.9 3.7 %copy-start.2 = (bf16[256,4096]{1,0:T(8,128)(2,1)S(1)}, bf16[256,4096]{1,0:T(8,128)(2,1)}, u32[]{:S(2)}) copy-start(bf16[256,4096]{1,0:T(8,128)(2,1)} %get-tuple-element.18) | copy-start | bytes 6291460

commit v2 on v1

--- a/solution.py
+++ b/solution.py
@@ -11,7 +11,7 @@
 MESH = pl.DeviceIdType.MESH
 LOW = -1e30
 TABLE_ROWS_AT = 64
-UNROLL = 4
+UNROLL = 8
 
 
 def flipped(me, d):
@@ -58,9 +58,9 @@
     stage,
     recv,
     push,
+    qs_ref,
     acc,
     m_ref,
-    l_ref,
     tsend,
     trecv,
     psend,
@@ -92,12 +92,12 @@
             device_id_type=MESH,
         )
 
-    def page_copy(d):
+    def page_copy(d, half):
         return pltpu.make_async_remote_copy(
-            src_ref=stage.at[d],
-            dst_ref=recv.at[:, pl.ds(pl.multiple_of(me * keys, keys), keys)],
-            send_sem=psend.at[d],
-            recv_sem=precv.at[d],
+            src_ref=stage.at[d, half],
+            dst_ref=recv.at[half, pl.ds(pl.multiple_of(me * keys, keys), keys)],
+            send_sem=psend.at[half, d],
+            recv_sem=precv.at[half, d],
             device_id={"pool": flipped(me, d)},
             device_id_type=MESH,
         )
@@ -133,14 +133,33 @@
 
         lax.fori_loop(0, rows, one, 0, unroll=True)
 
-    for d in order:
-
+    per_block = max(1, 256 // keys)
+    block = per_block * keys
+    far = list(range(n // 2, n))
+    near = list(range(1, n // 2))
+    queue = [(d, half) for d in far for half in range(2)]
+    window = min(len(queue), 3 * per_block)
+    ahead = list(range(n // 2, n // 2 + -(-window // 2)))
+
+    def gather_for(d):
         def to_stage(at, key_page, value_page):
             stage[d, 0, pl.ds(at, page_tok)] = key_page
             stage[d, 1, pl.ds(at, page_tok)] = value_page
 
         gather(flipped(me, d), to_stage)
-        page_copy(d).start()
+
+    for d in ahead:
+        gather_for(d)
+        for half in range(2):
+            if (d, half) in queue[:window]:
+                page_copy(d, half).start()
+    for d in near:
+        gather_for(d)
+        page_copy(d, 0).start()
+        page_copy(d, 1).start()
+    for d in far:
+        if d not in ahead:
+            gather_for(d)
 
     def to_own(at, key_page, value_page):
         base = pl.multiple_of(me * keys, keys)
@@ -164,81 +183,86 @@
 
     scale = math.log2(math.e) / math.sqrt(hd)
 
+    rows_q = UNROLL * span
+
+    def turn(c, carry):
+        qs_ref[pl.ds(pl.multiple_of(c * span, span), span)] = q_ref[
+            :, pl.ds(pl.multiple_of(c * hd, hd), hd)
+        ]
+        return carry
+
+    lax.fori_loop(0, heads, turn, 0)
+
     def attend(load_k, load_v, load_bias, first):
         def some_heads(i, carry):
-            for u in range(UNROLL):
-                c = i * UNROLL + u
-                h = lax.div(i * UNROLL, group)
-                col = pl.multiple_of(h * hd, hd)
-                q = q_ref[:, pl.ds(pl.multiple_of(c * hd, hd), hd)]
-                s = lax.dot_general(
-                    load_k(col), q, (((1,), (1,)), ((), ())), preferred_element_type=jnp.float32
-                )
-                s = s + load_bias()
-                top = jnp.max(s, axis=0, keepdims=True)
-                if not first:
-                    old = m_ref[c]
-                    top = jnp.maximum(old, top)
-                w = jnp.exp2((s - top) * scale)
-                part = jnp.sum(w.reshape(w.shape[0] // 8, 8, span), axis=0)
-                summed = lax.dot_general(
-                    load_v(col),
-                    w.astype(jnp.bfloat16),
-                    (((0,), (0,)), ((), ())),
-                    preferred_element_type=jnp.float32,
-                )
-                if first:
-                    l_ref[c] = part
-                    acc[c] = summed
-                else:
-                    fade = jnp.exp2((old - top) * scale)
-                    l_ref[c] = l_ref[c] * fade + part
-                    acc[c] = acc[c] * fade + summed
-                m_ref[c] = top
+            h = lax.div(i * UNROLL, group)
+            col = pl.multiple_of(h * hd, hd)
+            at = pl.ds(pl.multiple_of(i * rows_q, rows_q), rows_q)
+            k_now, v_now = load_k(col), load_v(col)
+            v_now = jnp.concatenate([v_now, jnp.ones_like(v_now)], axis=1)
+            s = lax.dot_general(
+                qs_ref[at], k_now, (((1,), (1,)), ((), ())), preferred_element_type=jnp.float32
+            )
+            s = s + load_bias()
+            top = jnp.broadcast_to(jnp.max(s, axis=1, keepdims=True), (rows_q, hd))
+            if not first:
+                old = m_ref[at]
+                top = jnp.maximum(old, top)
+            w = jnp.exp2((s - jnp.concatenate([top] * (s.shape[1] // hd), axis=1)) * scale)
+            summed = jnp.dot(w.astype(jnp.bfloat16), v_now, preferred_element_type=jnp.float32)
+            if not first:
+                fade = jnp.exp2((old - top) * scale)
+                summed = acc[at] * jnp.concatenate([fade, fade], axis=1) + summed
+            acc[at] = summed
+            m_ref[at] = top
             return carry
 
         lax.fori_loop(0, heads // UNROLL, some_heads, 0)
 
     def causal():
-        s_at = lax.broadcasted_iota(jnp.int32, (span, span), 0)
-        t_at = lax.broadcasted_iota(jnp.int32, (span, span), 1)
+        t_at = lax.rem(lax.broadcasted_iota(jnp.int32, (rows_q, span), 0), span)
+        s_at = lax.broadcasted_iota(jnp.int32, (rows_q, span), 1)
         return jnp.where(s_at <= t_at, 0.0, LOW)
 
     attend(lambda col: nk_ref[:, pl.ds(col, hd)], lambda col: nv_ref[:, pl.ds(col, hd)], causal, True)
 
-    per_block = max(1, 256 // keys)
-    block = per_block * keys
     own_block = lax.div(me, per_block)
-    done = {0}
-    for i in [0] + send_order(n // per_block):
+    sent = 0
+    for i in range(n // per_block):
+        for d in range(i * per_block, (i + 1) * per_block):
+            if d in far:
+                for _ in range(2):
+                    if sent + window < len(queue):
+                        page_copy(*queue[sent]).wait_send()
+                        page_copy(*queue[sent + window]).start()
+                        sent += 1
         for d in range(i * per_block, (i + 1) * per_block):
             if d:
-                page_copy(d).wait_recv()
+                page_copy(d, 0).wait_recv()
+                page_copy(d, 1).wait_recv()
         base = pl.multiple_of(flipped(own_block, i) * block, block)
-
-        def bias_block():
-            b = bias_ref[pl.ds(base, block), :]
-            return jnp.concatenate([b] * (span // b.shape[1]), axis=1)
 
         attend(
             lambda col: recv[0, pl.ds(base, block), pl.ds(col, hd)],
             lambda col: recv[1, pl.ds(base, block), pl.ds(col, hd)],
-            bias_block,
+            lambda: bias_ref[:, pl.ds(base, block)],
             False,
         )
 
     def finish(c, carry):
-        total = jnp.sum(l_ref[c], axis=0, keepdims=True)
-        value = acc[c] / total
-        out_ref[:, pl.ds(pl.multiple_of(c * hd, hd), hd)] = value.T.astype(jnp.bfloat16)
+        value = acc[pl.ds(pl.multiple_of(c * span, span), span)]
+        out_ref[:, pl.ds(pl.multiple_of(c * hd, hd), hd)] = (
+            value[:, :hd] / value[:, hd:]
+        ).astype(jnp.bfloat16)
         return carry
 
     lax.fori_loop(0, heads, finish, 0)
 
     for d in order:
         table_copy(d).wait_send()
-        page_copy(d).wait_send()
         row_copy(d).wait()
+    for d, half in queue[sent:] + [(d, half) for d in near for half in range(2)]:
+        page_copy(d, half).wait_send()
 
 
 def ranks(owner):
@@ -285,7 +309,7 @@
     )
     position = pages[:, None] * page_tok + jnp.arange(page_tok, dtype=jnp.int32)[None, :]
     bias = jnp.where(position.reshape(page_count * page_tok) < prefix_len[0], 0.0, LOW)
-    bias = jnp.broadcast_to(bias.astype(jnp.float32)[:, None], (page_count * page_tok, 128))
+    bias = bias.astype(jnp.float32)[None, :]
 
     d_owner, d_slot = dec_owner[0], dec_slot[0]
     d_rank = ranks(d_owner)
@@ -323,13 +347,13 @@
             pltpu.VMEM((n, 2, keys, columns), jnp.bfloat16),
             pltpu.VMEM((2, n * keys, columns), jnp.bfloat16),
             pltpu.VMEM((n, dec_pad, columns), jnp.bfloat16),
-            pltpu.VMEM((heads, hd, span), jnp.float32),
-            pltpu.VMEM((heads, 1, span), jnp.float32),
-            pltpu.VMEM((heads, 8, span), jnp.float32),
+            pltpu.VMEM((heads * span, hd), jnp.bfloat16),
+            pltpu.VMEM((heads * span, 2 * hd), jnp.float32),
+            pltpu.VMEM((heads * span, hd), jnp.float32),
             pltpu.SemaphoreType.DMA((n,)),
             pltpu.SemaphoreType.DMA((n,)),
-            pltpu.SemaphoreType.DMA((n,)),
-            pltpu.SemaphoreType.DMA((n,)),
+            pltpu.SemaphoreType.DMA((2, n)),
+            pltpu.SemaphoreType.DMA((2, n)),
             pltpu.SemaphoreType.DMA((n,)),
             pltpu.SemaphoreType.DMA((n,)),
             pltpu.SemaphoreType.DMA,

time: 172 us -> 137 us (0.80)
  Pallas kernels: 155 us -> 121 us
    pallas_call x1, Pallas kernels: 155 us -> 121 us  [shards(): pl.pallas_call(functools.partial(kernel, n, rows, page_tok, dec_rows, dec...]
where the time goes in v2:
time: 137 us; the launch traced here: 136 us
  Pallas kernels  121 us (88%)
  local copies, waits for them, and re-layouts  5.81 us (4%)
  other arithmetic  5.07 us (4%)
  matrix products  3.26 us (2%)
  between operations  1.37 us (1%)
    pallas_call x1, Pallas kernels, shards(): pl.pallas_call(functools.partial(kernel, n, rows, page_tok, dec_rows, dec...  121 us
    unnamed x9, local copies, waits for them, and re-layouts  3.23 us

profile of v2, /device:TPU:8, one launch (start us, length us, event | category | flops | bytes accessed | tf_op | source)
XLA Modules:
  0.0 136.3 jit_solution(10498159969322150105)
XLA Ops:
  1.3 0.9 convert_reduce_fusion.1
  2.2 0.7 fusion.8
  2.9 0.1 pad.1.clone
  2.9 0.1 pad.3.clone
  3.0 0.8 select_reduce_fusion.1
  3.8 0.9 convert_reduce_fusion
  4.7 0.7 multiply_add_fusion
  5.4 0.8 select_reduce_fusion
  6.2 0.1 reshape.65
  6.3 0.1 reshape.64
  6.4 0.1 add_add_fusion
  6.4 0.1 fusion.7
  6.5 0.1 select_n.36.bias_ref
  6.6 0.8 copy.21
  7.4 0.8 copy.22
  8.2 0.2 broadcast_in_dim.87
  8.4 0.2 broadcast_in_dim.86
  8.6 0.0 copy-start
  8.6 0.9 copy-done
  9.6 0.0 copy-start.1
  9.6 0.9 copy-done.1
  10.5 0.0 copy-start.3
  10.5 120.8 %shard_map.157 = (bf16[256,4096]{1,0:T(8,128)(2,1)}, bf16[8,64,512]{2,1,0:T(8,128)(2,1)S(1)}, s32[8,1,128]{2,1,0:T(1,128)S(1)}) custom-call(s32[8,1,128]{2,1,0:T(1,128)S(1)} %bitcast.23, s32[1,256]{1,0:T(1,128)S(1)} %get-tuple-element.13.placed_ref, bf16[256,4096]{1,0:T(8,128)(2,1)} %q_ref.1, bf16[256,512]{1,0:T(8,128)(2,1)S(1)} %copy-done, ...), custom_call_target="tpu_custom_call" | custom-call | flops 9663676416 | bytes 16777216 | tf_op jit(solution)/shard_map/pallas_call | solution.py:334
  131.3 0.0 copy-start.2
  131.3 0.1 slice_reduce_fusion
  131.4 0.1 eq.86
  131.5 0.2 fusion.2
  131.7 0.0 copy-done.3
  131.7 1.1 fusion
  132.8 2.2 %fusion.1 = bf16[512,512]{1,0:T(8,128)(2,1)} fusion(bf16[512,512]{1,0:T(8,128)(2,1)} %param.27, bf16[256,512]{1,0:T(8,128)(2,1)S(1)} %bitcast.24, pred[512]{0:T(512)(128)(4,1)S(1)} %fusion.2, s32[256]{0:T(256)S(1)} %eq.86), kind=kOutput, calls=%fused_computation.3 | convolution fusion | flops 134873088 | bytes 1312256 | tf_op jit(solution)/shard_map/dot_general | solution.py:395
  134.9 0.0 copy-done.2
  135.0 1.3 copy.25
  (4 shorter events, 0.0 us)
Async XLA Ops:
  8.6 1.0 copy-start
  9.6 0.9 copy-start.1
  10.5 121.2 %copy-start.3 = (bf16[512,512]{1,0:T(8,128)(2,1)S(1)}, bf16[512,512]{1,0:T(8,128)(2,1)}, u32[]{:S(2)}) copy-start(bf16[512,512]{1,0:T(8,128)(2,1)} %param.26) | copy-start | bytes 1572868
  131.3 3.7 %copy-start.2 = (bf16[256,4096]{1,0:T(8,128)(2,1)S(1)}, bf16[256,4096]{1,0:T(8,128)(2,1)}, u32[]{:S(2)}) copy-start(bf16[256,4096]{1,0:T(8,128)(2,1)} %get-tuple-element.18) | copy-start | bytes 6291460
